TPU v7x, 256 devices: a whole 4x4x8 slice. The times are simulated.
256 devices in a mesh: blk: 32 (over z, y_hi, core), rep: 8 (over x, y_lo).
Axes of the slice: x: 4, y: 4 (y_hi: 2, y_lo: 2; y = y_hi * 2 + y_lo), z: 8, core: 2. Of those that a mesh axis runs over, the one named last changes fastest.
Arguments:
- embeddings: float32 [32768, 768], P(('blk', 'rep')), may hold values from -48 to 48
- labels: float32 [32768, 128], P(('blk', 'rep')), may hold values from -6 to 6
Outputs:
- updated: float32 [32768, 128], P(('blk', 'rep'))
All inputs are finite; a program needn't handle non-finite values.
Results may differ from a plain program's by a relative error of at most 0.0003.
Values sent between devices are 32-bit elements; how exact they have to be, the bound alone decides.
A program may use at most 64 MiB of HBM per device.

v0:
```python
import math

import jax
import jax.numpy as jnp
from jax import lax
from jax.sharding import PartitionSpec as P


def passed_along(block, axis, distance):
    devices = range(lax.axis_size(axis))
    route = [((i - distance) % len(devices), i) for i in devices]
    return lax.ppermute(block, axis, route)


def combined_all(value, axis, combine):
    everything = jax.tree.map(lambda part: lax.all_gather(part, axis), value)
    leading = jax.tree.map(lambda part: part[0], everything)

    def hop(k, so_far):
        return combine(so_far, jax.tree.map(lambda part: part[k], everything))

    return lax.fori_loop(1, lax.axis_size(axis), hop, leading)


def combine(first, second):
    top_one, total_one, summed_one = first
    top_two, total_two, summed_two = second
    top_both = jnp.maximum(top_one, top_two)
    factor_one = jnp.exp(top_one - top_both)
    factor_two = jnp.exp(top_two - top_both)
    total_both = total_one * factor_one + total_two * factor_two
    summed_both = summed_one * factor_one[:, None] + summed_two * factor_two[:, None]
    return (top_both, total_both, summed_both)


def body(embeddings, labels):
    row_count, feature_width = embeddings.shape
    rep_count = lax.axis_size("rep")
    blk_count = lax.axis_size("blk")
    blk_index = lax.axis_index("blk")
    rep_index = lax.axis_index("rep")
    slab_rows = row_count * rep_count
    factor = 1.0 / math.sqrt(feature_width)
    own_block = jnp.concatenate([embeddings, labels], axis=1)

    def absorb(state, queries, query_ids, block, key_start):
        keys = block[:, :feature_width]
        values = block[:, feature_width:]
        scores = (
            lax.dot_general(
                keys,
                queries,
                (((1,), (1,)), ((), ())),
                precision=lax.Precision.HIGHEST,
                preferred_element_type=jnp.float32,
            )
            * factor
        )
        key_ids = key_start + jnp.arange(block.shape[0], dtype=jnp.int32)
        scores = jnp.where(key_ids[:, None] == query_ids[None, :], -jnp.inf, scores)
        top_old, total_old, summed_old = state
        top_new = jnp.maximum(top_old, jnp.max(scores, axis=0))
        rescale = jnp.exp(top_old - top_new)
        weights = jnp.exp(scores - top_new[None, :])
        total_new = total_old * rescale + jnp.sum(weights, axis=0)
        summed_new = summed_old * rescale[:, None] + lax.dot_general(
            weights,
            values,
            (((0,), (0,)), ((), ())),
            precision=lax.Precision.HIGHEST,
            preferred_element_type=jnp.float32,
        )
        return (top_new, total_new, summed_new)

    slab_queries = lax.all_gather(embeddings, "rep", axis=0, tiled=True)
    query_ids = blk_index * slab_rows + jnp.arange(slab_rows, dtype=jnp.int32)
    state = absorb(
        (
            jnp.full((slab_rows,), -1e30, jnp.float32),
            jnp.zeros((slab_rows,), jnp.float32),
            jnp.zeros((slab_rows, labels.shape[1]), jnp.float32),
        ),
        slab_queries,
        query_ids,
        own_block,
        (blk_index * rep_count + rep_index) * row_count,
    )

    def advance(turn, carried):
        partial_state, block = carried
        block = passed_along(block, "blk", 1)
        source = (blk_index - turn) % blk_count
        partial_state = absorb(
            partial_state,
            slab_queries,
            query_ids,
            block,
            (source * rep_count + rep_index) * row_count,
        )
        return (partial_state, block)

    state, own_block = lax.fori_loop(1, blk_count, advance, (state, own_block))
    top_score, total, summed = state
    top_score, total, summed = combined_all((top_score, total, summed), "rep", combine)
    own_total = lax.dynamic_slice_in_dim(total, rep_index * row_count, row_count, 0)
    own_summed = lax.dynamic_slice_in_dim(summed, rep_index * row_count, row_count, 0)
    propagated = own_summed / own_total[:, None]
    return 0.1 * labels + 0.9 * propagated


def solution(mesh):
    placed = (P(("blk", "rep"), None), P(("blk", "rep"), None))
    return jax.shard_map(
        body, mesh=mesh, in_specs=placed, out_specs=P(("blk", "rep"), None), check_vma=False
    )
```

profile of v0, /device:TPU:1, one launch (start us, length us, event | category | flops | bytes accessed | tf_op | source)
XLA Modules:
  0.0 855.6 jit_solution(11523323178625506846)
XLA Ops:
  9.2 76.4 %all-gather.6.cloned.1.call-done = f32[1024,768]{1,0:T(8,128)} async-done(((f32[128,768]{1,0:T(8,128)}), f32[1024,768]{1,0:T(8,128)}) %all-gather.6.cloned.1.call-update) | async-done | bytes 3145744 | tf_op jit(solution)/shard_map/all_gather | solution.py:75
  85.6 5.5 fusion.13
  93.1 640.3 %while.42 = (s32[]{:T(128)}, f32[1024]{0:T(1024)S(1)}, f32[1024]{0:T(1024)S(1)}, f32[1024,128]{1,0:T(8,128)}, f32[128,896]{1,0:T(8,128)}, /*index=5*/s32[]{:T(12...) while((s32[]{:T(128)}, f32[1024]{0:T(1024)S(1)}, ...), condition=%wide.region_5.6_spmd.clone, body=%wide.region_2.5_spmd.clone.sunk | while | flops 1410468992 | bytes 13247890 | solution.py:102
  96.7 5.7 collective-permute-done
  102.4 4.4 fusion.26
  115.6 5.7 collective-permute-done
  134.4 5.7 collective-permute-done
  153.3 5.7 collective-permute-done
  172.1 7.1 collective-permute-done
  179.2 4.4 fusion.26
  191.0 9.2 %collective-permute-done = f32[128,896]{1,0:T(8,128)} collective-permute-done((f32[128,896]{1,0:T(8,128)}, f32[128,896]{1,0:T(8,128)}, u32[]{:S(2)}, u32[]{:S(2)}) %collective-permute-start) | collective-permute-done | bytes 458784 | tf_op jit(solution)/shard_map/while/body/eval_jaxpr/ppermute | solution.py:12
  200.2 4.4 fusion.26
  209.8 11.3 %collective-permute-done = f32[128,896]{1,0:T(8,128)} collective-permute-done((f32[128,896]{1,0:T(8,128)}, f32[128,896]{1,0:T(8,128)}, u32[]{:S(2)}, u32[]{:S(2)}) %collective-permute-start) | collective-permute-done | bytes 458784 | tf_op jit(solution)/shard_map/while/body/eval_jaxpr/ppermute | solution.py:12
  221.2 4.4 fusion.26
  230.3 11.8 %collective-permute-done = f32[128,896]{1,0:T(8,128)} collective-permute-done((f32[128,896]{1,0:T(8,128)}, f32[128,896]{1,0:T(8,128)}, u32[]{:S(2)}, u32[]{:S(2)}) %collective-permute-start) | collective-permute-done | bytes 458784 | tf_op jit(solution)/shard_map/while/body/eval_jaxpr/ppermute | solution.py:12
  242.1 4.4 fusion.26
  251.3 11.8 %collective-permute-done = f32[128,896]{1,0:T(8,128)} collective-permute-done((f32[128,896]{1,0:T(8,128)}, f32[128,896]{1,0:T(8,128)}, u32[]{:S(2)}, u32[]{:S(2)}) %collective-permute-start) | collective-permute-done | bytes 458784 | tf_op jit(solution)/shard_map/while/body/eval_jaxpr/ppermute | solution.py:12
  263.1 4.4 fusion.26
  272.2 11.8 %collective-permute-done = f32[128,896]{1,0:T(8,128)} collective-permute-done((f32[128,896]{1,0:T(8,128)}, f32[128,896]{1,0:T(8,128)}, u32[]{:S(2)}, u32[]{:S(2)}) %collective-permute-start) | collective-permute-done | bytes 458784 | tf_op jit(solution)/shard_map/while/body/eval_jaxpr/ppermute | solution.py:12
  284.0 4.4 fusion.26
  293.2 11.8 %collective-permute-done = f32[128,896]{1,0:T(8,128)} collective-permute-done((f32[128,896]{1,0:T(8,128)}, f32[128,896]{1,0:T(8,128)}, u32[]{:S(2)}, u32[]{:S(2)}) %collective-permute-start) | collective-permute-done | bytes 458784 | tf_op jit(solution)/shard_map/while/body/eval_jaxpr/ppermute | solution.py:12
  305.0 4.4 fusion.26
  314.1 11.8 %collective-permute-done = f32[128,896]{1,0:T(8,128)} collective-permute-done((f32[128,896]{1,0:T(8,128)}, f32[128,896]{1,0:T(8,128)}, u32[]{:S(2)}, u32[]{:S(2)}) %collective-permute-start) | collective-permute-done | bytes 458784 | tf_op jit(solution)/shard_map/while/body/eval_jaxpr/ppermute | solution.py:12
  326.0 4.4 fusion.26
  335.1 11.8 %collective-permute-done = f32[128,896]{1,0:T(8,128)} collective-permute-done((f32[128,896]{1,0:T(8,128)}, f32[128,896]{1,0:T(8,128)}, u32[]{:S(2)}, u32[]{:S(2)}) %collective-permute-start) | collective-permute-done | bytes 458784 | tf_op jit(solution)/shard_map/while/body/eval_jaxpr/ppermute | solution.py:12
  346.9 4.4 fusion.26
  356.1 11.8 %collective-permute-done = f32[128,896]{1,0:T(8,128)} collective-permute-done((f32[128,896]{1,0:T(8,128)}, f32[128,896]{1,0:T(8,128)}, u32[]{:S(2)}, u32[]{:S(2)}) %collective-permute-start) | collective-permute-done | bytes 458784 | tf_op jit(solution)/shard_map/while/body/eval_jaxpr/ppermute | solution.py:12
  377.0 11.8 %collective-permute-done = f32[128,896]{1,0:T(8,128)} collective-permute-done((f32[128,896]{1,0:T(8,128)}, f32[128,896]{1,0:T(8,128)}, u32[]{:S(2)}, u32[]{:S(2)}) %collective-permute-start) | collective-permute-done | bytes 458784 | tf_op jit(solution)/shard_map/while/body/eval_jaxpr/ppermute | solution.py:12
  398.0 11.8 %collective-permute-done = f32[128,896]{1,0:T(8,128)} collective-permute-done((f32[128,896]{1,0:T(8,128)}, f32[128,896]{1,0:T(8,128)}, u32[]{:S(2)}, u32[]{:S(2)}) %collective-permute-start) | collective-permute-done | bytes 458784 | tf_op jit(solution)/shard_map/while/body/eval_jaxpr/ppermute | solution.py:12
  418.9 11.8 %collective-permute-done = f32[128,896]{1,0:T(8,128)} collective-permute-done((f32[128,896]{1,0:T(8,128)}, f32[128,896]{1,0:T(8,128)}, u32[]{:S(2)}, u32[]{:S(2)}) %collective-permute-start) | collective-permute-done | bytes 458784 | tf_op jit(solution)/shard_map/while/body/eval_jaxpr/ppermute | solution.py:12
  439.9 11.8 %collective-permute-done = f32[128,896]{1,0:T(8,128)} collective-permute-done((f32[128,896]{1,0:T(8,128)}, f32[128,896]{1,0:T(8,128)}, u32[]{:S(2)}, u32[]{:S(2)}) %collective-permute-start) | collective-permute-done | bytes 458784 | tf_op jit(solution)/shard_map/while/body/eval_jaxpr/ppermute | solution.py:12
  460.9 11.8 %collective-permute-done = f32[128,896]{1,0:T(8,128)} collective-permute-done((f32[128,896]{1,0:T(8,128)}, f32[128,896]{1,0:T(8,128)}, u32[]{:S(2)}, u32[]{:S(2)}) %collective-permute-start) | collective-permute-done | bytes 458784 | tf_op jit(solution)/shard_map/while/body/eval_jaxpr/ppermute | solution.py:12
  481.8 11.8 %collective-permute-done = f32[128,896]{1,0:T(8,128)} collective-permute-done((f32[128,896]{1,0:T(8,128)}, f32[128,896]{1,0:T(8,128)}, u32[]{:S(2)}, u32[]{:S(2)}) %collective-permute-start) | collective-permute-done | bytes 458784 | tf_op jit(solution)/shard_map/while/body/eval_jaxpr/ppermute | solution.py:12
  502.8 11.8 %collective-permute-done = f32[128,896]{1,0:T(8,128)} collective-permute-done((f32[128,896]{1,0:T(8,128)}, f32[128,896]{1,0:T(8,128)}, u32[]{:S(2)}, u32[]{:S(2)}) %collective-permute-start) | collective-permute-done | bytes 458784 | tf_op jit(solution)/shard_map/while/body/eval_jaxpr/ppermute | solution.py:12
  523.7 11.8 %collective-permute-done = f32[128,896]{1,0:T(8,128)} collective-permute-done((f32[128,896]{1,0:T(8,128)}, f32[128,896]{1,0:T(8,128)}, u32[]{:S(2)}, u32[]{:S(2)}) %collective-permute-start) | collective-permute-done | bytes 458784 | tf_op jit(solution)/shard_map/while/body/eval_jaxpr/ppermute | solution.py:12
  544.7 11.8 %collective-permute-done = f32[128,896]{1,0:T(8,128)} collective-permute-done((f32[128,896]{1,0:T(8,128)}, f32[128,896]{1,0:T(8,128)}, u32[]{:S(2)}, u32[]{:S(2)}) %collective-permute-start) | collective-permute-done | bytes 458784 | tf_op jit(solution)/shard_map/while/body/eval_jaxpr/ppermute | solution.py:12
  565.7 11.8 %collective-permute-done = f32[128,896]{1,0:T(8,128)} collective-permute-done((f32[128,896]{1,0:T(8,128)}, f32[128,896]{1,0:T(8,128)}, u32[]{:S(2)}, u32[]{:S(2)}) %collective-permute-start) | collective-permute-done | bytes 458784 | tf_op jit(solution)/shard_map/while/body/eval_jaxpr/ppermute | solution.py:12
  586.6 11.8 %collective-permute-done = f32[128,896]{1,0:T(8,128)} collective-permute-done((f32[128,896]{1,0:T(8,128)}, f32[128,896]{1,0:T(8,128)}, u32[]{:S(2)}, u32[]{:S(2)}) %collective-permute-start) | collective-permute-done | bytes 458784 | tf_op jit(solution)/shard_map/while/body/eval_jaxpr/ppermute | solution.py:12
  607.6 11.8 %collective-permute-done = f32[128,896]{1,0:T(8,128)} collective-permute-done((f32[128,896]{1,0:T(8,128)}, f32[128,896]{1,0:T(8,128)}, u32[]{:S(2)}, u32[]{:S(2)}) %collective-permute-start) | collective-permute-done | bytes 458784 | tf_op jit(solution)/shard_map/while/body/eval_jaxpr/ppermute | solution.py:12
  628.5 11.8 %collective-permute-done = f32[128,896]{1,0:T(8,128)} collective-permute-done((f32[128,896]{1,0:T(8,128)}, f32[128,896]{1,0:T(8,128)}, u32[]{:S(2)}, u32[]{:S(2)}) %collective-permute-start) | collective-permute-done | bytes 458784 | tf_op jit(solution)/shard_map/while/body/eval_jaxpr/ppermute | solution.py:12
  649.5 11.8 %collective-permute-done = f32[128,896]{1,0:T(8,128)} collective-permute-done((f32[128,896]{1,0:T(8,128)}, f32[128,896]{1,0:T(8,128)}, u32[]{:S(2)}, u32[]{:S(2)}) %collective-permute-start) | collective-permute-done | bytes 458784 | tf_op jit(solution)/shard_map/while/body/eval_jaxpr/ppermute | solution.py:12
  670.5 11.8 %collective-permute-done = f32[128,896]{1,0:T(8,128)} collective-permute-done((f32[128,896]{1,0:T(8,128)}, f32[128,896]{1,0:T(8,128)}, u32[]{:S(2)}, u32[]{:S(2)}) %collective-permute-start) | collective-permute-done | bytes 458784 | tf_op jit(solution)/shard_map/while/body/eval_jaxpr/ppermute | solution.py:12
  691.4 11.8 %collective-permute-done = f32[128,896]{1,0:T(8,128)} collective-permute-done((f32[128,896]{1,0:T(8,128)}, f32[128,896]{1,0:T(8,128)}, u32[]{:S(2)}, u32[]{:S(2)}) %collective-permute-start) | collective-permute-done | bytes 458784 | tf_op jit(solution)/shard_map/while/body/eval_jaxpr/ppermute | solution.py:12
  712.4 11.8 %collective-permute-done = f32[128,896]{1,0:T(8,128)} collective-permute-done((f32[128,896]{1,0:T(8,128)}, f32[128,896]{1,0:T(8,128)}, u32[]{:S(2)}, u32[]{:S(2)}) %collective-permute-start) | collective-permute-done | bytes 458784 | tf_op jit(solution)/shard_map/while/body/eval_jaxpr/ppermute | solution.py:12
  733.3 21.9 %all-gather = f32[8192]{0:T(1024)S(1)} all-gather(f32[1024]{0:T(1024)S(1)} %get-tuple-element.405), channel_id=2, replica_groups=mesh['blk'=32,'rep'=8] {'rep'}, dimensions={0}, use_global_device_ids=true | all-gather | bytes 36864 | tf_op jit(solution)/shard_map/all_gather | solution.py:16
  755.2 27.9 %all-gather.1 = f32[8192]{0:T(1024)S(1)} all-gather(f32[1024]{0:T(1024)S(1)} %get-tuple-element.406), channel_id=3, replica_groups=mesh['blk'=32,'rep'=8] {'rep'}, dimensions={0}, use_global_device_ids=true | all-gather | bytes 36864 | tf_op jit(solution)/shard_map/all_gather | solution.py:16
  783.2 52.8 %all-gather.8.cloned.1.call-done = f32[8192,128]{1,0:T(8,128)} async-done(((f32[1024,128]{1,0:T(8,128)}), f32[8192,128]{1,0:T(8,128)}) %all-gather.8.cloned.1.call-update) | async-done | bytes 4194320 | tf_op jit(solution)/shard_map/all_gather | solution.py:16
  837.0 10.9 %while.41 = (s32[]{:T(128)}, f32[1024]{0:T(1024)S(1)}, f32[1024]{0:T(1024)S(1)}, f32[1024,128]{1,0:T(8,128)S(1)}, f32[8,1024]{1,0:T(8,128)S(1)}, /*index=5*/f32[...) while((s32[]{:T(128)}, f32[1024]{0:T(1024)S(1)}, f32[1024]{0:T(1024)S(1)}, ...), condition=%wide.region_7.8_spmd, body=%wide.region_6.7_spmd.sunk | while | flops 399365 | bytes 1630359 | solution.py:22
  (467 shorter events, 277.7 us)
Async XLA Ops:
  6.5 84.7 %copy-start.3 = (f32[128,128]{1,0:T(8,128)S(1)}, f32[128,128]{1,0:T(8,128)}, u32[]{:S(2)}) copy-start(f32[128,128]{1,0:T(8,128)} %param.7) | copy-start | bytes 196612
  6.5 79.1 %all-gather.6.cloned.1.call-start = ((), (), s32[]{:S(2)}) async-start(), calls=%async_computation | async-start | bytes 3538944 | tf_op jit(solution)/shard_map/all_gather | solution.py:75
  7.3 828.7 %all-gather.8.cloned.1.call-start = ((), (), s32[]{:S(2)}) async-start(), calls=%async_computation.1 | async-start | bytes 4718592 | tf_op jit(solution)/shard_map/all_gather | solution.py:16
  93.1 9.4 %collective-permute-start = (f32[128,896]{1,0:T(8,128)}, f32[128,896]{1,0:T(8,128)}, u32[]{:S(2)}, u32[]{:S(2)}) collective-permute-start(f32[128,896]{1,0:T(8,128)} %get-tuple-element.614), channel_id=1, source_target_pairs={{248,0},{0,8},{8,16},{16,24},{24,32},{32,40},{40,48},{48,56},{56,6... | collective-permute-start | bytes 1376264 | tf_op jit(solution)/shard_map/while/body/eval_jaxpr/ppermute | solution.py:12
  111.6 9.7 %collective-permute-start = (f32[128,896]{1,0:T(8,128)}, f32[128,896]{1,0:T(8,128)}, u32[]{:S(2)}, u32[]{:S(2)}) collective-permute-start(f32[128,896]{1,0:T(8,128)} %get-tuple-element.614), channel_id=1, source_target_pairs={{248,0},{0,8},{8,16},{16,24},{24,32},{32,40},{40,48},{48,56},{56,6... | collective-permute-start | bytes 1376264 | tf_op jit(solution)/shard_map/while/body/eval_jaxpr/ppermute | solution.py:12
  130.4 9.7 %collective-permute-start = (f32[128,896]{1,0:T(8,128)}, f32[128,896]{1,0:T(8,128)}, u32[]{:S(2)}, u32[]{:S(2)}) collective-permute-start(f32[128,896]{1,0:T(8,128)} %get-tuple-element.614), channel_id=1, source_target_pairs={{248,0},{0,8},{8,16},{16,24},{24,32},{32,40},{40,48},{48,56},{56,6... | collective-permute-start | bytes 1376264 | tf_op jit(solution)/shard_map/while/body/eval_jaxpr/ppermute | solution.py:12
  149.3 9.7 %collective-permute-start = (f32[128,896]{1,0:T(8,128)}, f32[128,896]{1,0:T(8,128)}, u32[]{:S(2)}, u32[]{:S(2)}) collective-permute-start(f32[128,896]{1,0:T(8,128)} %get-tuple-element.614), channel_id=1, source_target_pairs={{248,0},{0,8},{8,16},{16,24},{24,32},{32,40},{40,48},{48,56},{56,6... | collective-permute-start | bytes 1376264 | tf_op jit(solution)/shard_map/while/body/eval_jaxpr/ppermute | solution.py:12
  168.1 11.1 %collective-permute-start = (f32[128,896]{1,0:T(8,128)}, f32[128,896]{1,0:T(8,128)}, u32[]{:S(2)}, u32[]{:S(2)}) collective-permute-start(f32[128,896]{1,0:T(8,128)} %get-tuple-element.614), channel_id=1, source_target_pairs={{248,0},{0,8},{8,16},{16,24},{24,32},{32,40},{40,48},{48,56},{56,6... | collective-permute-start | bytes 1376264 | tf_op jit(solution)/shard_map/while/body/eval_jaxpr/ppermute | solution.py:12
  188.4 11.8 %collective-permute-start = (f32[128,896]{1,0:T(8,128)}, f32[128,896]{1,0:T(8,128)}, u32[]{:S(2)}, u32[]{:S(2)}) collective-permute-start(f32[128,896]{1,0:T(8,128)} %get-tuple-element.614), channel_id=1, source_target_pairs={{248,0},{0,8},{8,16},{16,24},{24,32},{32,40},{40,48},{48,56},{56,6... | collective-permute-start | bytes 1376264 | tf_op jit(solution)/shard_map/while/body/eval_jaxpr/ppermute | solution.py:12
  209.3 11.8 %collective-permute-start = (f32[128,896]{1,0:T(8,128)}, f32[128,896]{1,0:T(8,128)}, u32[]{:S(2)}, u32[]{:S(2)}) collective-permute-start(f32[128,896]{1,0:T(8,128)} %get-tuple-element.614), channel_id=1, source_target_pairs={{248,0},{0,8},{8,16},{16,24},{24,32},{32,40},{40,48},{48,56},{56,6... | collective-permute-start | bytes 1376264 | tf_op jit(solution)/shard_map/while/body/eval_jaxpr/ppermute | solution.py:12
  230.3 11.8 %collective-permute-start = (f32[128,896]{1,0:T(8,128)}, f32[128,896]{1,0:T(8,128)}, u32[]{:S(2)}, u32[]{:S(2)}) collective-permute-start(f32[128,896]{1,0:T(8,128)} %get-tuple-element.614), channel_id=1, source_target_pairs={{248,0},{0,8},{8,16},{16,24},{24,32},{32,40},{40,48},{48,56},{56,6... | collective-permute-start | bytes 1376264 | tf_op jit(solution)/shard_map/while/body/eval_jaxpr/ppermute | solution.py:12
  230.3 18.2 %copy-start.1 = (f32[1024,128]{1,0:T(8,128)S(1)}, f32[1024,128]{1,0:T(8,128)}, u32[]{:S(2)}) copy-start(f32[1024,128]{1,0:T(8,128)} %get-tuple-element.613) | copy-start | bytes 1572868 | tf_op jit(solution)/shard_map/while
  251.2 11.8 %collective-permute-start = (f32[128,896]{1,0:T(8,128)}, f32[128,896]{1,0:T(8,128)}, u32[]{:S(2)}, u32[]{:S(2)}) collective-permute-start(f32[128,896]{1,0:T(8,128)} %get-tuple-element.614), channel_id=1, source_target_pairs={{248,0},{0,8},{8,16},{16,24},{24,32},{32,40},{40,48},{48,56},{56,6... | collective-permute-start | bytes 1376264 | tf_op jit(solution)/shard_map/while/body/eval_jaxpr/ppermute | solution.py:12
  251.2 18.2 %copy-start.1 = (f32[1024,128]{1,0:T(8,128)S(1)}, f32[1024,128]{1,0:T(8,128)}, u32[]{:S(2)}) copy-start(f32[1024,128]{1,0:T(8,128)} %get-tuple-element.613) | copy-start | bytes 1572868 | tf_op jit(solution)/shard_map/while
  272.2 11.8 %collective-permute-start = (f32[128,896]{1,0:T(8,128)}, f32[128,896]{1,0:T(8,128)}, u32[]{:S(2)}, u32[]{:S(2)}) collective-permute-start(f32[128,896]{1,0:T(8,128)} %get-tuple-element.614), channel_id=1, source_target_pairs={{248,0},{0,8},{8,16},{16,24},{24,32},{32,40},{40,48},{48,56},{56,6... | collective-permute-start | bytes 1376264 | tf_op jit(solution)/shard_map/while/body/eval_jaxpr/ppermute | solution.py:12
  272.2 18.2 %copy-start.1 = (f32[1024,128]{1,0:T(8,128)S(1)}, f32[1024,128]{1,0:T(8,128)}, u32[]{:S(2)}) copy-start(f32[1024,128]{1,0:T(8,128)} %get-tuple-element.613) | copy-start | bytes 1572868 | tf_op jit(solution)/shard_map/while
  293.2 11.8 %collective-permute-start = (f32[128,896]{1,0:T(8,128)}, f32[128,896]{1,0:T(8,128)}, u32[]{:S(2)}, u32[]{:S(2)}) collective-permute-start(f32[128,896]{1,0:T(8,128)} %get-tuple-element.614), channel_id=1, source_target_pairs={{248,0},{0,8},{8,16},{16,24},{24,32},{32,40},{40,48},{48,56},{56,6... | collective-permute-start | bytes 1376264 | tf_op jit(solution)/shard_map/while/body/eval_jaxpr/ppermute | solution.py:12
  293.2 18.2 %copy-start.1 = (f32[1024,128]{1,0:T(8,128)S(1)}, f32[1024,128]{1,0:T(8,128)}, u32[]{:S(2)}) copy-start(f32[1024,128]{1,0:T(8,128)} %get-tuple-element.613) | copy-start | bytes 1572868 | tf_op jit(solution)/shard_map/while
  314.1 11.8 %collective-permute-start = (f32[128,896]{1,0:T(8,128)}, f32[128,896]{1,0:T(8,128)}, u32[]{:S(2)}, u32[]{:S(2)}) collective-permute-start(f32[128,896]{1,0:T(8,128)} %get-tuple-element.614), channel_id=1, source_target_pairs={{248,0},{0,8},{8,16},{16,24},{24,32},{32,40},{40,48},{48,56},{56,6... | collective-permute-start | bytes 1376264 | tf_op jit(solution)/shard_map/while/body/eval_jaxpr/ppermute | solution.py:12
  314.1 18.2 %copy-start.1 = (f32[1024,128]{1,0:T(8,128)S(1)}, f32[1024,128]{1,0:T(8,128)}, u32[]{:S(2)}) copy-start(f32[1024,128]{1,0:T(8,128)} %get-tuple-element.613) | copy-start | bytes 1572868 | tf_op jit(solution)/shard_map/while
  335.1 11.8 %collective-permute-start = (f32[128,896]{1,0:T(8,128)}, f32[128,896]{1,0:T(8,128)}, u32[]{:S(2)}, u32[]{:S(2)}) collective-permute-start(f32[128,896]{1,0:T(8,128)} %get-tuple-element.614), channel_id=1, source_target_pairs={{248,0},{0,8},{8,16},{16,24},{24,32},{32,40},{40,48},{48,56},{56,6... | collective-permute-start | bytes 1376264 | tf_op jit(solution)/shard_map/while/body/eval_jaxpr/ppermute | solution.py:12
  335.1 18.2 %copy-start.1 = (f32[1024,128]{1,0:T(8,128)S(1)}, f32[1024,128]{1,0:T(8,128)}, u32[]{:S(2)}) copy-start(f32[1024,128]{1,0:T(8,128)} %get-tuple-element.613) | copy-start | bytes 1572868 | tf_op jit(solution)/shard_map/while
  356.0 11.8 %collective-permute-start = (f32[128,896]{1,0:T(8,128)}, f32[128,896]{1,0:T(8,128)}, u32[]{:S(2)}, u32[]{:S(2)}) collective-permute-start(f32[128,896]{1,0:T(8,128)} %get-tuple-element.614), channel_id=1, source_target_pairs={{248,0},{0,8},{8,16},{16,24},{24,32},{32,40},{40,48},{48,56},{56,6... | collective-permute-start | bytes 1376264 | tf_op jit(solution)/shard_map/while/body/eval_jaxpr/ppermute | solution.py:12
  356.0 18.2 %copy-start.1 = (f32[1024,128]{1,0:T(8,128)S(1)}, f32[1024,128]{1,0:T(8,128)}, u32[]{:S(2)}) copy-start(f32[1024,128]{1,0:T(8,128)} %get-tuple-element.613) | copy-start | bytes 1572868 | tf_op jit(solution)/shard_map/while
  377.0 11.8 %collective-permute-start = (f32[128,896]{1,0:T(8,128)}, f32[128,896]{1,0:T(8,128)}, u32[]{:S(2)}, u32[]{:S(2)}) collective-permute-start(f32[128,896]{1,0:T(8,128)} %get-tuple-element.614), channel_id=1, source_target_pairs={{248,0},{0,8},{8,16},{16,24},{24,32},{32,40},{40,48},{48,56},{56,6... | collective-permute-start | bytes 1376264 | tf_op jit(solution)/shard_map/while/body/eval_jaxpr/ppermute | solution.py:12
  377.0 18.2 %copy-start.1 = (f32[1024,128]{1,0:T(8,128)S(1)}, f32[1024,128]{1,0:T(8,128)}, u32[]{:S(2)}) copy-start(f32[1024,128]{1,0:T(8,128)} %get-tuple-element.613) | copy-start | bytes 1572868 | tf_op jit(solution)/shard_map/while
  398.0 11.8 %collective-permute-start = (f32[128,896]{1,0:T(8,128)}, f32[128,896]{1,0:T(8,128)}, u32[]{:S(2)}, u32[]{:S(2)}) collective-permute-start(f32[128,896]{1,0:T(8,128)} %get-tuple-element.614), channel_id=1, source_target_pairs={{248,0},{0,8},{8,16},{16,24},{24,32},{32,40},{40,48},{48,56},{56,6... | collective-permute-start | bytes 1376264 | tf_op jit(solution)/shard_map/while/body/eval_jaxpr/ppermute | solution.py:12
  398.0 18.2 %copy-start.1 = (f32[1024,128]{1,0:T(8,128)S(1)}, f32[1024,128]{1,0:T(8,128)}, u32[]{:S(2)}) copy-start(f32[1024,128]{1,0:T(8,128)} %get-tuple-element.613) | copy-start | bytes 1572868 | tf_op jit(solution)/shard_map/while
  418.9 11.8 %collective-permute-start = (f32[128,896]{1,0:T(8,128)}, f32[128,896]{1,0:T(8,128)}, u32[]{:S(2)}, u32[]{:S(2)}) collective-permute-start(f32[128,896]{1,0:T(8,128)} %get-tuple-element.614), channel_id=1, source_target_pairs={{248,0},{0,8},{8,16},{16,24},{24,32},{32,40},{40,48},{48,56},{56,6... | collective-permute-start | bytes 1376264 | tf_op jit(solution)/shard_map/while/body/eval_jaxpr/ppermute | solution.py:12
  418.9 18.2 %copy-start.1 = (f32[1024,128]{1,0:T(8,128)S(1)}, f32[1024,128]{1,0:T(8,128)}, u32[]{:S(2)}) copy-start(f32[1024,128]{1,0:T(8,128)} %get-tuple-element.613) | copy-start | bytes 1572868 | tf_op jit(solution)/shard_map/while
  439.9 11.8 %collective-permute-start = (f32[128,896]{1,0:T(8,128)}, f32[128,896]{1,0:T(8,128)}, u32[]{:S(2)}, u32[]{:S(2)}) collective-permute-start(f32[128,896]{1,0:T(8,128)} %get-tuple-element.614), channel_id=1, source_target_pairs={{248,0},{0,8},{8,16},{16,24},{24,32},{32,40},{40,48},{48,56},{56,6... | collective-permute-start | bytes 1376264 | tf_op jit(solution)/shard_map/while/body/eval_jaxpr/ppermute | solution.py:12
  439.9 18.2 %copy-start.1 = (f32[1024,128]{1,0:T(8,128)S(1)}, f32[1024,128]{1,0:T(8,128)}, u32[]{:S(2)}) copy-start(f32[1024,128]{1,0:T(8,128)} %get-tuple-element.613) | copy-start | bytes 1572868 | tf_op jit(solution)/shard_map/while
  460.8 11.8 %collective-permute-start = (f32[128,896]{1,0:T(8,128)}, f32[128,896]{1,0:T(8,128)}, u32[]{:S(2)}, u32[]{:S(2)}) collective-permute-start(f32[128,896]{1,0:T(8,128)} %get-tuple-element.614), channel_id=1, source_target_pairs={{248,0},{0,8},{8,16},{16,24},{24,32},{32,40},{40,48},{48,56},{56,6... | collective-permute-start | bytes 1376264 | tf_op jit(solution)/shard_map/while/body/eval_jaxpr/ppermute | solution.py:12
  460.8 18.2 %copy-start.1 = (f32[1024,128]{1,0:T(8,128)S(1)}, f32[1024,128]{1,0:T(8,128)}, u32[]{:S(2)}) copy-start(f32[1024,128]{1,0:T(8,128)} %get-tuple-element.613) | copy-start | bytes 1572868 | tf_op jit(solution)/shard_map/while
  481.8 11.8 %collective-permute-start = (f32[128,896]{1,0:T(8,128)}, f32[128,896]{1,0:T(8,128)}, u32[]{:S(2)}, u32[]{:S(2)}) collective-permute-start(f32[128,896]{1,0:T(8,128)} %get-tuple-element.614), channel_id=1, source_target_pairs={{248,0},{0,8},{8,16},{16,24},{24,32},{32,40},{40,48},{48,56},{56,6... | collective-permute-start | bytes 1376264 | tf_op jit(solution)/shard_map/while/body/eval_jaxpr/ppermute | solution.py:12
  481.8 18.2 %copy-start.1 = (f32[1024,128]{1,0:T(8,128)S(1)}, f32[1024,128]{1,0:T(8,128)}, u32[]{:S(2)}) copy-start(f32[1024,128]{1,0:T(8,128)} %get-tuple-element.613) | copy-start | bytes 1572868 | tf_op jit(solution)/shard_map/while
  502.8 11.8 %collective-permute-start = (f32[128,896]{1,0:T(8,128)}, f32[128,896]{1,0:T(8,128)}, u32[]{:S(2)}, u32[]{:S(2)}) collective-permute-start(f32[128,896]{1,0:T(8,128)} %get-tuple-element.614), channel_id=1, source_target_pairs={{248,0},{0,8},{8,16},{16,24},{24,32},{32,40},{40,48},{48,56},{56,6... | collective-permute-start | bytes 1376264 | tf_op jit(solution)/shard_map/while/body/eval_jaxpr/ppermute | solution.py:12
  502.8 18.2 %copy-start.1 = (f32[1024,128]{1,0:T(8,128)S(1)}, f32[1024,128]{1,0:T(8,128)}, u32[]{:S(2)}) copy-start(f32[1024,128]{1,0:T(8,128)} %get-tuple-element.613) | copy-start | bytes 1572868 | tf_op jit(solution)/shard_map/while
  523.7 11.8 %collective-permute-start = (f32[128,896]{1,0:T(8,128)}, f32[128,896]{1,0:T(8,128)}, u32[]{:S(2)}, u32[]{:S(2)}) collective-permute-start(f32[128,896]{1,0:T(8,128)} %get-tuple-element.614), channel_id=1, source_target_pairs={{248,0},{0,8},{8,16},{16,24},{24,32},{32,40},{40,48},{48,56},{56,6... | collective-permute-start | bytes 1376264 | tf_op jit(solution)/shard_map/while/body/eval_jaxpr/ppermute | solution.py:12
  544.7 11.8 %collective-permute-start = (f32[128,896]{1,0:T(8,128)}, f32[128,896]{1,0:T(8,128)}, u32[]{:S(2)}, u32[]{:S(2)}) collective-permute-start(f32[128,896]{1,0:T(8,128)} %get-tuple-element.614), channel_id=1, source_target_pairs={{248,0},{0,8},{8,16},{16,24},{24,32},{32,40},{40,48},{48,56},{56,6... | collective-permute-start | bytes 1376264 | tf_op jit(solution)/shard_map/while/body/eval_jaxpr/ppermute | solution.py:12
  565.6 11.8 %collective-permute-start = (f32[128,896]{1,0:T(8,128)}, f32[128,896]{1,0:T(8,128)}, u32[]{:S(2)}, u32[]{:S(2)}) collective-permute-start(f32[128,896]{1,0:T(8,128)} %get-tuple-element.614), channel_id=1, source_target_pairs={{248,0},{0,8},{8,16},{16,24},{24,32},{32,40},{40,48},{48,56},{56,6... | collective-permute-start | bytes 1376264 | tf_op jit(solution)/shard_map/while/body/eval_jaxpr/ppermute | solution.py:12
  586.6 11.8 %collective-permute-start = (f32[128,896]{1,0:T(8,128)}, f32[128,896]{1,0:T(8,128)}, u32[]{:S(2)}, u32[]{:S(2)}) collective-permute-start(f32[128,896]{1,0:T(8,128)} %get-tuple-element.614), channel_id=1, source_target_pairs={{248,0},{0,8},{8,16},{16,24},{24,32},{32,40},{40,48},{48,56},{56,6... | collective-permute-start | bytes 1376264 | tf_op jit(solution)/shard_map/while/body/eval_jaxpr/ppermute | solution.py:12
  607.6 11.8 %collective-permute-start = (f32[128,896]{1,0:T(8,128)}, f32[128,896]{1,0:T(8,128)}, u32[]{:S(2)}, u32[]{:S(2)}) collective-permute-start(f32[128,896]{1,0:T(8,128)} %get-tuple-element.614), channel_id=1, source_target_pairs={{248,0},{0,8},{8,16},{16,24},{24,32},{32,40},{40,48},{48,56},{56,6... | collective-permute-start | bytes 1376264 | tf_op jit(solution)/shard_map/while/body/eval_jaxpr/ppermute | solution.py:12
  628.5 11.8 %collective-permute-start = (f32[128,896]{1,0:T(8,128)}, f32[128,896]{1,0:T(8,128)}, u32[]{:S(2)}, u32[]{:S(2)}) collective-permute-start(f32[128,896]{1,0:T(8,128)} %get-tuple-element.614), channel_id=1, source_target_pairs={{248,0},{0,8},{8,16},{16,24},{24,32},{32,40},{40,48},{48,56},{56,6... | collective-permute-start | bytes 1376264 | tf_op jit(solution)/shard_map/while/body/eval_jaxpr/ppermute | solution.py:12
  649.5 11.8 %collective-permute-start = (f32[128,896]{1,0:T(8,128)}, f32[128,896]{1,0:T(8,128)}, u32[]{:S(2)}, u32[]{:S(2)}) collective-permute-start(f32[128,896]{1,0:T(8,128)} %get-tuple-element.614), channel_id=1, source_target_pairs={{248,0},{0,8},{8,16},{16,24},{24,32},{32,40},{40,48},{48,56},{56,6... | collective-permute-start | bytes 1376264 | tf_op jit(solution)/shard_map/while/body/eval_jaxpr/ppermute | solution.py:12
  670.4 11.8 %collective-permute-start = (f32[128,896]{1,0:T(8,128)}, f32[128,896]{1,0:T(8,128)}, u32[]{:S(2)}, u32[]{:S(2)}) collective-permute-start(f32[128,896]{1,0:T(8,128)} %get-tuple-element.614), channel_id=1, source_target_pairs={{248,0},{0,8},{8,16},{16,24},{24,32},{32,40},{40,48},{48,56},{56,6... | collective-permute-start | bytes 1376264 | tf_op jit(solution)/shard_map/while/body/eval_jaxpr/ppermute | solution.py:12
  691.4 11.8 %collective-permute-start = (f32[128,896]{1,0:T(8,128)}, f32[128,896]{1,0:T(8,128)}, u32[]{:S(2)}, u32[]{:S(2)}) collective-permute-start(f32[128,896]{1,0:T(8,128)} %get-tuple-element.614), channel_id=1, source_target_pairs={{248,0},{0,8},{8,16},{16,24},{24,32},{32,40},{40,48},{48,56},{56,6... | collective-permute-start | bytes 1376264 | tf_op jit(solution)/shard_map/while/body/eval_jaxpr/ppermute | solution.py:12
  712.4 11.8 %collective-permute-start = (f32[128,896]{1,0:T(8,128)}, f32[128,896]{1,0:T(8,128)}, u32[]{:S(2)}, u32[]{:S(2)}) collective-permute-start(f32[128,896]{1,0:T(8,128)} %get-tuple-element.614), channel_id=1, source_target_pairs={{248,0},{0,8},{8,16},{16,24},{24,32},{32,40},{40,48},{48,56},{56,6... | collective-permute-start | bytes 1376264 | tf_op jit(solution)/shard_map/while/body/eval_jaxpr/ppermute | solution.py:12
  (49 other events, 309.3 us)
Sparse Core Ops, SparseCore 0:
  9.1 76.4 all-gather.5
  733.5 102.4 all-gather.7
where the time goes:
time: 861 us; the launch traced here: 856 us
  waiting for transfers between devices  464 us (54%)
  matrix products  204 us (24%)
  local copies, waits for them, and re-layouts  82.4 us (10%)
  blocking collectives  49.8 us (6%)
  starting transfers between devices  22.8 us (3%)
  other arithmetic  16.9 us (2%)
  between operations  13.5 us (2%)
    ppermute x31, waiting for transfers between devices, passed_along(): return lax.ppermute(block, axis, route)  334 us
    dot_general x32, matrix products, absorb(): lax.dot_general(keys, queries, (((1,), (1,)), ((), ())), precision=lax.Pr...  142 us
    while x186, local copies, waits for them, and re-layouts  81.1 us
    all_gather x1, waiting for transfers between devices, body(): slab_queries = lax.all_gather(embeddings, 'rep', axis=0, tiled=True)  76.4 us
    dot_general x32, matrix products, absorb(): lax.dot_general(weights, values, (((0,), (0,)), ((), ())), precision=lax....  62.6 us
    all_gather x1, waiting for transfers between devices, combined_all(): everything = jax.tree.map(lambda part: lax.all_gather(part, axis), value)  52.8 us
    all_gather x2, blocking collectives, combined_all(): everything = jax.tree.map(lambda part: lax.all_gather(part, axis), value)  49.8 us
    ppermute x31, starting transfers between devices, passed_along(): return lax.ppermute(block, axis, route)  22.8 us
  transfers between devices with their start and end apart: 33, of which 33 were waited for; matrix products, arithmetic and copies ran while one was open for 0% of the time, Pallas kernels for 0%

commit v1 on v0

v1 whole, which is shorter than its diff:
```python
import math

import jax
import jax.numpy as jnp
from jax import lax
from jax.experimental import pallas as pl
from jax.experimental.pallas import tpu as pltpu
from jax.sharding import PartitionSpec as P

MESH = pl.DeviceIdType.MESH
F32, BF16 = jnp.float32, jnp.bfloat16
ROWS, DIM, LAB = 128, 768, 128
GQ, UK = 512, 256
NG, NU = 4, 8
NEG = -1e30
NT = (((1,), (1,)), ((), ()))
NN = (((1,), (0,)), ((), ()))

BLOCKS = [
    (1, 0), (3, 0), (0, 1), (0, 3),
    (1, 1), (1, 3), (3, 1), (3, 3),
    (0, 0), (2, 0), (0, 2), (1, 2),
    (3, 2), (2, 1), (2, 3), (2, 2),
]
SLOT = {block: i for i, block in enumerate(BLOCKS)}
OWN = SLOT[(0, 0)]
LINKS = [("x", 1), ("x", -1), ("y", 1), ("y", -1)]

ORDER = [('kc', 0), ('q', 0), ('z', 1), ('kc', 1), ('q', 1), ('qc', 0), ('t', 0, 0), ('z', 2), ('t', 0, 1), ('q', 2), ('kc', 2), ('t', 0, 2), ('q', 3), ('z', 3), ('q', 4), ('kc', 3), ('t', 0, 3), ('z', 4), ('q', 5), ('qc', 1), ('t', 1, 0), ('kc', 4), ('t', 1, 1), ('t', 1, 2), ('z', 5), ('t', 1, 3), ('q', 6), ('t', 0, 4), ('t', 1, 4), ('kc', 5), ('q', 7), ('qc', 2), ('t', 2, 0), ('t', 2, 1), ('z', 6), ('q', 8), ('t', 2, 2), ('t', 2, 3), ('q', 9), ('kc', 6), ('qc', 3), ('t', 3, 0), ('t', 3, 1), ('z', 7), ('t', 3, 2), ('t', 3, 3), ('t', 2, 4), ('kc', 7), ('t', 3, 4), ('t', 3, 5), ('t', 3, 6), ('t', 3, 7), ('f', 3), ('t', 1, 5), ('t', 1, 6), ('t', 1, 7), ('f', 1), ('t', 0, 5), ('t', 0, 6), ('t', 0, 7), ('f', 0), ('t', 2, 5), ('t', 2, 6), ('t', 2, 7), ('f', 2)]


def split_order(order):
    tiles, before, after, waiting = [], [], {}, []
    for item in order:
        if item[0] == "t":
            tiles.append((item[1], item[2]))
            before.append(waiting)
            waiting = []
        elif item[0] == "f":
            after[len(tiles) - 1] = item[1]
        else:
            waiting.append(item)
    return tiles, before, after


def pick(i, values):
    out = jnp.int32(values[0])
    for j in range(1, len(values)):
        if values[j] != values[j - 1]:
            out = jnp.where(i >= j, jnp.int32(values[j]), out)
    return out


def device(x, y, z, c):
    return ((z * 2 + y // 2) * 2 + c, x * 2 + lax.rem(y, 2))


def kernel(emb, lab, out, qf, kf, qh, ql, kh, kl, vt, s_buf, acc, m_ref, l_ref, back,
           q_send, q_recv, z_send, z_recv, d_send, d_recv, b_send, b_recv):
    blk, rep = lax.axis_index("blk"), lax.axis_index("rep")
    mx, my = rep // 2, lax.rem(blk // 2, 2) * 2 + lax.rem(rep, 2)
    mz, mc = blk // 4, lax.rem(blk, 2)

    def at(dx=0, dy=0, dz=0, dc=0):
        return device(lax.rem(mx + dx % 4, 4), lax.rem(my + dy % 4, 4), lax.rem(mz + dz % 8, 8), lax.rem(mc + dc, 2))

    barrier = pltpu.get_barrier_semaphore()
    peers = [at(dx=b[0], dy=b[1]) for b in BLOCKS if b != (0, 0)] + [at(dz=1), at(dz=-1), at(dc=1)]
    for peer in peers:
        pl.semaphore_signal(barrier, inc=1, device_id=peer, device_id_type=MESH)
    kf[0, :ROWS, :DIM] = emb[...]
    kf[0, :ROWS, DIM:] = lab[...]
    qf[OWN] = emb[...]
    m_ref[...] = jnp.full_like(m_ref, NEG)
    l_ref[...] = jnp.zeros_like(l_ref)
    acc[...] = jnp.zeros_like(acc)
    pl.semaphore_wait(barrier, len(peers))

    def remote(src, dst, send, recv, to):
        return pltpu.make_async_remote_copy(
            src_ref=src, dst_ref=dst, send_sem=send, recv_sem=recv, device_id=to, device_id_type=MESH
        )

    def plane(link, n):
        axis, sign = LINKS[link]
        near, far = ((0, 64), (64, 64)) if axis == "x" else ((64, 64), (0, 64))
        half = 0 if sign == 1 else 32
        near_part, far_part = (near[0] + half, 32), (far[0] + half, 32)
        along, across, part = [
            (0, 0, near), (0, 0, far), (-sign, 0, near_part), (-sign, 0, far_part),
            (0, 1, far), (0, -1, far), (0, 2, far),
            (-sign, 1, far_part), (-sign, -1, far_part), (-sign, 2, far_part),
        ][n]
        here, there = (along, across), (along - sign, across)
        step = (sign, 0)
        if axis == "y":
            here, there, step = here[::-1], there[::-1], step[::-1]
        mine = SLOT[(here[0] % 4, here[1] % 4)]
        theirs = SLOT[(there[0] % 4, there[1] % 4)]
        rows = pl.ds(part[0], part[1])
        return remote(qf.at[mine, rows], qf.at[theirs, rows], q_send.at[link, n], q_recv.at[link, n],
                      at(dx=step[0], dy=step[1]))

    def ring(way, r):
        sign = 1 if way == 0 else -1
        theirs = pl.ds(64 * way, 64)
        if r == 1:
            src = kf.at[0, pl.ds(64 * way, 64)]
        elif r == 2:
            src = kf.at[0, pl.ds(64 - 64 * way, 64)]
        else:
            src = kf.at[r - 2, theirs]
        return remote(src, kf.at[r, theirs], z_send.at[way, r], z_recv.at[way, r], at(dz=sign))

    def across(u):
        return remote(kf.at[u, pl.ds(0, ROWS)], kf.at[u, pl.ds(ROWS, ROWS)], d_send.at[u], d_recv.at[u], at(dc=1))

    def home(slot):
        dx, dy = BLOCKS[slot]
        return remote(acc.at[slot], back.at[slot], b_send.at[slot], b_recv.at[slot], at(dx=dx, dy=dy))

    for n in range(2):
        for link in range(4):
            plane(link, n).start()
        for way in range(2):
            ring(way, n + 1).start()
    across(0).start()

    scale = math.log2(math.e) / math.sqrt(DIM)

    def convert_queries(g):
        for b in range(4):
            slot = 4 * g + b

            def chunk(i, carry, slot=slot):
                rows = pl.ds(pl.multiple_of(i * 32, 32), 32)
                value = qf[slot, rows, :] * scale
                high = value.astype(BF16)
                to = pl.ds(pl.multiple_of(slot * ROWS + i * 32, 32), 32)
                qh[to, :] = high
                ql[to, :] = (value - high.astype(F32)).astype(BF16)
                return carry

            lax.fori_loop(0, ROWS // 32, chunk, 0)

    def convert_keys(u):
        def chunk(i, carry):
            rows = pl.ds(pl.multiple_of(i * 32, 32), 32)
            value = kf[u, rows, :DIM]
            high = value.astype(BF16)
            to = pl.ds(pl.multiple_of(u * UK + i * 32, 32), 32)
            kh[to, :] = high
            kl[to, :] = (value - high.astype(F32)).astype(BF16)
            return carry

        lax.fori_loop(0, UK // 32, chunk, 0)
        value = kf[u, :, DIM:].T
        high = value.astype(BF16)
        vt[:LAB, u * UK:(u + 1) * UK] = high
        vt[LAB:, u * UK:(u + 1) * UK] = (value - high.astype(F32)).astype(BF16)

    def event(item):
        kind, n = item
        if kind == "q":
            for link in range(4):
                plane(link, n).wait_recv()
            if n + 2 < 10:
                for link in range(4):
                    plane(link, n + 2).start()
        elif kind == "z":
            for way in range(2):
                ring(way, n).wait_recv()
                if n + 2 < NU:
                    ring(way, n + 2).start()
            across(n).start()
        elif kind == "kc":
            across(n).wait_recv()
            convert_keys(n)
        else:
            convert_queries(n)

    def finish(g):
        for b in range(4):
            slot = 4 * g + b
            acc[slot, LAB:LAB + 1, :] = m_ref[g, :, b * ROWS:(b + 1) * ROWS]
            acc[slot, LAB + 1:LAB + 2, :] = l_ref[g, :, b * ROWS:(b + 1) * ROWS]
            if slot != OWN:
                home(slot).start()

    def scores(g, u):
        queries = pl.ds(pl.multiple_of(g * GQ, GQ), GQ)
        keys = pl.ds(pl.multiple_of(u * UK, UK), UK)
        a, b = kh[keys, :], qh[queries, :]
        s = lax.dot_general(a, b, NT, preferred_element_type=F32)
        s += lax.dot_general(kl[keys, :], b, NT, preferred_element_type=F32)
        s += lax.dot_general(a, ql[queries, :], NT, preferred_element_type=F32)
        return s

    def absorb(g, u, s):
        keys = pl.ds(pl.multiple_of(u * UK, UK), UK)
        m_old = m_ref[g]
        m_new = jnp.maximum(m_old, jnp.max(s, axis=0, keepdims=True))
        shrink = jnp.exp2(m_old - m_new)
        p = jnp.exp2(s - m_new)
        m_ref[g] = m_new
        l_ref[g] = l_ref[g] * shrink + jnp.sum(p, axis=0, keepdims=True)
        high = p.astype(BF16)
        low = (p - high.astype(F32)).astype(BF16)
        v = vt[:, keys]
        o = lax.dot_general(v, high, NN, preferred_element_type=F32)
        o = o[:LAB] + o[LAB:] + lax.dot_general(v[:LAB], low, NN, preferred_element_type=F32)
        for b in range(4):
            cols = slice(b * ROWS, (b + 1) * ROWS)
            acc[g * 4 + b, :LAB, :] = acc[g * 4 + b, :LAB, :] * shrink[:, cols] + o[:, cols]

    def exclude_self(g, u, slot):
        @pl.when((g == OWN // 4) & (u == 0))
        def _():
            block = s_buf[slot, :ROWS, (OWN % 4) * ROWS:(OWN % 4 + 1) * ROWS]
            same = lax.broadcasted_iota(jnp.int32, block.shape, 0) == lax.broadcasted_iota(jnp.int32, block.shape, 1)
            s_buf[slot, :ROWS, (OWN % 4) * ROWS:(OWN % 4 + 1) * ROWS] = jnp.where(same, NEG, block)

    tiles, before, after = split_order(ORDER)
    groups, units = [t[0] for t in tiles], [t[1] for t in tiles]
    count = len(tiles)

    def when_step(j, parity, table, act):
        for step in range(parity, count - 2, 2):
            if table(step):
                @pl.when(j == step)
                def _(step=step):
                    act(step)

    def act_before(step):
        for item in before[step + 1]:
            event(item)

    for item in before[0]:
        event(item)
    s_buf[0] = scores(groups[0], units[0])
    exclude_self(groups[0], units[0], 0)

    def body(i, carry):
        for parity in range(2):
            j = 2 * i + parity
            when_step(j, parity, lambda step: before[step + 1], act_before)
            g, u = pick(j, groups), pick(j, units)
            g_next, u_next = pick(j + 1, groups), pick(j + 1, units)
            following = scores(g_next, u_next)
            absorb(g, u, s_buf[parity])
            s_buf[1 - parity] = following
            exclude_self(g_next, u_next, 1 - parity)
            when_step(j, parity, lambda step: step in after, lambda step: finish(after[step]))
        return carry

    lax.fori_loop(0, (count - 2) // 2, body, 0)
    for item in before[count - 1]:
        event(item)
    following = scores(groups[-1], units[-1])
    absorb(groups[-2], units[-2], s_buf[0])
    s_buf[1] = following
    if count - 2 in after:
        finish(after[count - 2])
    absorb(groups[-1], units[-1], s_buf[1])
    finish(after[count - 1])

    others = [s for s in range(len(BLOCKS)) if s != OWN]
    for slot in others:
        home(slot).wait_recv()
    top = acc[OWN, LAB:LAB + 1, :]
    for slot in others:
        top = jnp.maximum(top, back[slot, LAB:LAB + 1, :])
    total = jnp.zeros_like(top)
    summed = jnp.zeros((LAB, ROWS), F32)
    for slot in range(len(BLOCKS)):
        ref = acc if slot == OWN else back
        weight = jnp.exp2(ref[slot, LAB:LAB + 1, :] - top)
        total += weight * ref[slot, LAB + 1:LAB + 2, :]
        summed += weight * ref[slot, :LAB, :]
    out[...] = 0.1 * lab[...] + 0.9 * (summed / total).T

    for n in range(10):
        for link in range(4):
            plane(link, n).wait_send()
    for r in range(1, NU):
        for way in range(2):
            ring(way, r).wait_send()
    for u in range(NU):
        across(u).wait_send()
    for slot in others:
        home(slot).wait_send()


def body(embeddings, labels):
    vmem = pl.BlockSpec(memory_space=pltpu.VMEM)
    return pl.pallas_call(
        kernel,
        out_shape=jax.ShapeDtypeStruct((ROWS, LAB), F32),
        in_specs=[vmem, vmem],
        out_specs=vmem,
        scratch_shapes=[
            pltpu.VMEM((16, ROWS, DIM), F32),
            pltpu.VMEM((NU, UK, DIM + LAB), F32),
            pltpu.VMEM((NG * GQ, DIM), BF16),
            pltpu.VMEM((NG * GQ, DIM), BF16),
            pltpu.VMEM((NU * UK, DIM), BF16),
            pltpu.VMEM((NU * UK, DIM), BF16),
            pltpu.VMEM((2 * LAB, NU * UK), BF16),
            pltpu.VMEM((2, UK, GQ), F32),
            pltpu.VMEM((16, LAB + 8, ROWS), F32),
            pltpu.VMEM((NG, 1, GQ), F32),
            pltpu.VMEM((NG, 1, GQ), F32),
            pltpu.VMEM((16, LAB + 8, ROWS), F32),
            pltpu.SemaphoreType.DMA((4, 10)),
            pltpu.SemaphoreType.DMA((4, 10)),
            pltpu.SemaphoreType.DMA((2, NU)),
            pltpu.SemaphoreType.DMA((2, NU)),
            pltpu.SemaphoreType.DMA((NU,)),
            pltpu.SemaphoreType.DMA((NU,)),
            pltpu.SemaphoreType.DMA((16,)),
            pltpu.SemaphoreType.DMA((16,)),
        ],
        compiler_params=pltpu.CompilerParams(
            collective_id=0, has_side_effects=True, vmem_limit_bytes=56 * 2**20
        ),
        name="propagate",
    )(embeddings, labels)


def solution(mesh):
    placed = P(("blk", "rep"), None)
    return jax.shard_map(body, mesh=mesh, in_specs=(placed, placed), out_specs=placed, check_vma=False)
```

time: 861 us -> 76.8 us (0.09)
  waiting for transfers between devices: 464 us -> 0 us
  matrix products: 204 us -> 0 us
  local copies, waits for them, and re-layouts: 82.4 us -> 1.47 us
  Pallas kernels: 0 us -> 75.2 us
  blocking collectives: 49.8 us -> 0 us
  starting transfers between devices: 22.8 us -> 0 us
  other arithmetic: 16.9 us -> 0 us
  between operations: 13.5 us -> 0.01 us
    ppermute x31 -> x0, waiting for transfers between devices: 334 us -> none  [passed_along(): return lax.ppermute(block, axis, route)]
    dot_general x64 -> x0, matrix products: 204 us -> none  [the longest x32 142 us: absorb(): lax.dot_general(keys, queries, (((1,), (1,)), ((), ())), precision=lax.Pr...]
    all_gather x2 -> x0, waiting for transfers between devices: 129 us -> none  [the longest x1 76.4 us: body(): slab_queries = lax.all_gather(embeddings, 'rep', axis=0, tiled=True)]
    while x186 -> x0, local copies, waits for them, and re-layouts: 81.1 us -> none
    pallas_call x0 -> x1, Pallas kernels: none -> 75.2 us  [body(): pl.pallas_call(kernel, out_shape=jax.ShapeDtypeStruct((ROWS, LAB), F32),...]
    all_gather x2 -> x0, blocking collectives: 49.8 us -> none  [combined_all(): everything = jax.tree.map(lambda part: lax.all_gather(part, axis), value)]
    ppermute x31 -> x0, starting transfers between devices: 22.8 us -> none  [passed_along(): return lax.ppermute(block, axis, route)]
    add x110 -> x0, other arithmetic: 11.9 us -> none  [the longest x7 10.5 us: combine(): summed_one * factor_one[:, None] + summed_two * factor_two[:, None]]
  transfers between devices with their start and end apart: 33 -> 0, of which waited for: 33 -> 0; matrix products, arithmetic and copies ran while one was open for 0% -> 0% of each run, Pallas kernels for 0% -> 0%
where the time goes in v1:
time: 76.8 us; the launch traced here: 76.7 us
  Pallas kernels  75.2 us (98%)
  local copies, waits for them, and re-layouts  1.47 us (2%)
    pallas_call x1, Pallas kernels, body(): pl.pallas_call(kernel, out_shape=jax.ShapeDtypeStruct((ROWS, LAB), F32),...  75.2 us

profile of v1, /device:TPU:1, one launch (start us, length us, event | category | flops | bytes accessed | tf_op | source)
XLA Modules:
  0.0 76.7 jit_solution(690992749222043055)
XLA Ops:
  0.0 75.2 %propagate.1 = f32[128,128]{1,0:T(8,128)} custom-call(f32[128,768]{1,0:T(8,128)} %emb.1, f32[128,128]{1,0:T(8,128)} %lab.1), custom_call_target="tpu_custom_call" | custom-call | tf_op jit(solution)/shard_map/propagate/pallas_call | solution.py:296
  75.2 1.5 %copy.4 = f32[128,128]{1,0:T(8,128)} copy(f32[128,128]{1,0:T(8,128)} %propagate.1) | data formatting | bytes 131072

commit v2 on v1

v2 whole, which is shorter than its diff:
```python
import math

import jax
import jax.numpy as jnp
from jax import lax
from jax.experimental import pallas as pl
from jax.experimental.pallas import tpu as pltpu
from jax.sharding import PartitionSpec as P

MESH = pl.DeviceIdType.MESH
F32, BF16 = jnp.float32, jnp.bfloat16
ROWS, DIM, LAB = 128, 768, 128
GQ, UK = 512, 512
NG, NU = 4, 4
RING, NR = 256, 8
NEG = -1e30
NT = (((1,), (1,)), ((), ()))
NN = (((1,), (0,)), ((), ()))

HALVES = [
    (1, 0, 0), (1, 0, 1), (3, 0, 0), (3, 0, 1), (0, 1, 0), (0, 1, 1), (0, 3, 0), (0, 3, 1),
    (0, 0, 0), (0, 0, 1), (2, 0, 0), (2, 0, 1), (0, 2, 0), (0, 2, 1), (1, 1, 0), (1, 1, 1),
    (3, 3, 0), (3, 3, 1), (1, 3, 0), (1, 3, 1), (3, 1, 0), (3, 1, 1), (2, 1, 0), (1, 2, 1),
    (1, 2, 0), (2, 1, 1), (3, 2, 0), (3, 2, 1), (2, 3, 0), (2, 3, 1), (2, 2, 0), (2, 2, 1),
]
BLOCKS = sorted({half[:2] for half in HALVES})
SLOT = {block: i for i, block in enumerate(BLOCKS)}
OWN = SLOT[(0, 0)]
OWN_GROUP, OWN_COL = HALVES.index((0, 0, 0)) // 8, HALVES.index((0, 0, 0)) % 8 * 64
FIRST = {(1, 1): (0, 1), (3, 3): (0, 3), (1, 3): (1, 0), (3, 1): (3, 0), (1, 2): (0, 2), (3, 2): (0, 2), (2, 1): (2, 0), (2, 3): (2, 0)}
ADDED = {(1, 0): [(1, 1), (1, 2)], (3, 0): [(3, 3), (3, 2)], (0, 1): [(3, 1), (2, 1)], (0, 3): [(1, 3), (2, 3)]}
DIRECT = [(2, 0), (0, 2), (2, 2)]
LINKS = [("x", 1), ("x", -1), ("y", 1), ("y", -1)]

ORDER = [
    ("kc", 0), ("q", 0), ("z", 1), ("kc", 1), ("q", 1), ("qc", 0), ("t", 0, 0), ("z", 2), ("q", 2), ("kc", 2),
    ("q", 3), ("z", 3), ("q", 4), ("qc", 1), ("kc", 3), ("t", 1, 0), ("t", 0, 1), ("z", 4), ("t", 1, 1), ("q", 5),
    ("kc", 4), ("q", 6), ("qc", 2), ("z", 5), ("t", 2, 0), ("kc", 5), ("q", 7), ("t", 2, 1), ("t", 0, 2), ("q", 8),
    ("z", 6), ("t", 1, 2), ("q", 9), ("kc", 6), ("qc", 3), ("t", 3, 0), ("t", 3, 1), ("z", 7), ("t", 3, 2),
    ("kc", 7), ("t", 3, 3), ("f", 3), ("t", 1, 3), ("f", 1), ("t", 2, 2), ("t", 2, 3), ("f", 2), ("t", 0, 3),
    ("f", 0),
]


def split_order(order):
    tiles, before, after, waiting = [], [], {}, []
    for item in order:
        if item[0] == "t":
            tiles.append((item[1], item[2]))
            before.append(waiting)
            waiting = []
        elif item[0] == "f":
            after[len(tiles) - 1] = item[1]
        else:
            waiting.append(item)
    return tiles, before, after


def pick(i, values):
    out = jnp.int32(values[0])
    for j in range(1, len(values)):
        if values[j] != values[j - 1]:
            out = jnp.where(i >= j, jnp.int32(values[j]), out)
    return out


def device(x, y, z, c):
    return ((z * 2 + y // 2) * 2 + c, x * 2 + lax.rem(y, 2))


def kernel(emb, lab, out, qf, kf, qh, ql, kh, kl, vt, s_buf, acc, m_ref, l_ref, state, back,
           in_sem, q_send, q_recv, z_send, z_recv, d_send, d_recv, b_send, b_recv):
    blk, rep = lax.axis_index("blk"), lax.axis_index("rep")
    mx, my = rep // 2, lax.rem(blk // 2, 2) * 2 + lax.rem(rep, 2)
    mz, mc = blk // 4, lax.rem(blk, 2)

    def at(dx=0, dy=0, dz=0, dc=0):
        return device(lax.rem(mx + dx % 4, 4), lax.rem(my + dy % 4, 4), lax.rem(mz + dz % 8, 8), lax.rem(mc + dc, 2))

    barrier = pltpu.get_barrier_semaphore()
    peers = [at(dx=b[0], dy=b[1]) for b in [*ADDED, *DIRECT]] + [at(dz=1), at(dz=-1), at(dc=1)]
    for peer in peers:
        pl.semaphore_signal(barrier, inc=1, device_id=peer, device_id_type=MESH)
    own = [
        pltpu.make_async_copy(emb, kf.at[0, pl.ds(0, ROWS), pl.ds(0, DIM)], in_sem.at[0]),
        pltpu.make_async_copy(lab, kf.at[0, pl.ds(0, ROWS), pl.ds(DIM, LAB)], in_sem.at[1]),
    ]
    for copy in own:
        copy.start()
    m_ref[...] = jnp.full_like(m_ref, NEG)
    l_ref[...] = jnp.zeros_like(l_ref)
    acc[...] = jnp.zeros_like(acc)
    for copy in own:
        copy.wait()
    qf[OWN] = kf[0, :ROWS, :DIM] * (math.log2(math.e) / math.sqrt(DIM))
    pl.semaphore_wait(barrier, len(peers))

    def remote(src, dst, send, recv, to):
        return pltpu.make_async_remote_copy(
            src_ref=src, dst_ref=dst, send_sem=send, recv_sem=recv, device_id=to, device_id_type=MESH
        )

    def plane(link, n):
        axis, sign = LINKS[link]
        near, far = ((0, 64), (64, 64)) if axis == "x" else ((64, 64), (0, 64))
        half = 0 if sign == 1 else 32
        near_part, far_part = (near[0] + half, 32), (far[0] + half, 32)
        along, across, part = [
            (0, 0, near), (0, 0, far), (-sign, 0, near_part), (-sign, 0, far_part),
            (0, 1, far), (0, -1, far), (0, 2, far),
            (-sign, 1, far_part), (-sign, -1, far_part), (-sign, 2, far_part),
        ][n]
        here, there = (along, across), (along - sign, across)
        step = (sign, 0)
        if axis == "y":
            here, there, step = here[::-1], there[::-1], step[::-1]
        mine = SLOT[(here[0] % 4, here[1] % 4)]
        theirs = SLOT[(there[0] % 4, there[1] % 4)]
        rows = pl.ds(part[0], part[1])
        return remote(qf.at[mine, rows], qf.at[theirs, rows], q_send.at[link, n], q_recv.at[link, n],
                      at(dx=step[0], dy=step[1]))

    def ring(way, r):
        sign = 1 if way == 0 else -1
        theirs = pl.ds(64 * way, 64)
        if r == 1:
            src = kf.at[0, pl.ds(64 * way, 64)]
        elif r == 2:
            src = kf.at[0, pl.ds(64 - 64 * way, 64)]
        else:
            src = kf.at[r - 2, theirs]
        return remote(src, kf.at[r, theirs], z_send.at[way, r], z_recv.at[way, r], at(dz=sign))

    def across(way, r):
        return remote(kf.at[r, pl.ds(64 * way, 64)], kf.at[r, pl.ds(ROWS + 64 * way, 64)],
                      d_send.at[way, r], d_recv.at[way, r], at(dc=1))

    def home(slot):
        dx, dy = FIRST.get(BLOCKS[slot], BLOCKS[slot])
        return remote(state.at[slot], back.at[slot], b_send.at[slot], b_recv.at[slot], at(dx=dx, dy=dy))

    for n in range(2):
        for link in range(4):
            plane(link, n).start()
        for way in range(2):
            ring(way, n + 1).start()
    for way in range(2):
        across(way, 0).start()

    def halves(value):
        high = value.astype(BF16)
        return high, (value - high.astype(F32)).astype(BF16)

    def convert_queries(g):
        for i in range(8 * g, 8 * g + 8):
            dx, dy, half = HALVES[i]
            rows = pl.ds(i * 64, 64)
            qh[rows, :], ql[rows, :] = halves(qf[SLOT[(dx, dy)], half * 64:half * 64 + 64])

    def convert_keys(r):
        for start in range(0, RING, ROWS):
            rows = pl.ds(r * RING + start, ROWS)
            kh[rows, :], kl[rows, :] = halves(kf[r, start:start + ROWS, :DIM])
        cols = pl.ds(r * RING, RING)
        vt[:LAB, cols], vt[LAB:, cols] = halves(kf[r, :, DIM:].T)

    def event(item):
        kind, n = item
        if kind == "q":
            for link in range(4):
                plane(link, n).wait_recv()
            if n + 2 < 10:
                for link in range(4):
                    plane(link, n + 2).start()
        elif kind == "z":
            for way in range(2):
                ring(way, n).wait_recv()
                if n + 2 < NR:
                    ring(way, n + 2).start()
                across(way, n).start()
        elif kind == "kc":
            for way in range(2):
                across(way, n).wait_recv()
            convert_keys(n)
        else:
            convert_queries(n)

    def finish(g):
        for pair in range(4):
            first, second = (SLOT[HALVES[8 * g + 2 * pair + h][:2]] for h in range(2))
            cols = slice(pair * ROWS, (pair + 1) * ROWS)
            for rows, value in (
                (slice(0, LAB), acc[g, :, cols]),
                (slice(LAB, LAB + 1), m_ref[g, :, cols]),
                (slice(LAB + 1, LAB + 2), l_ref[g, :, cols]),
            ):
                if first == second:
                    state[first, rows, :] = value
                else:
                    state[first, rows, :64] = value[:, :64]
                    state[second, rows, 64:] = value[:, 64:]
        for slot in complete[g]:
            home(slot).start()

    def scores(g, u):
        queries = pl.ds(pl.multiple_of(g * GQ, GQ), GQ)
        keys = pl.ds(pl.multiple_of(u * UK, UK), UK)
        a, b = kh[keys, :], qh[queries, :]
        s = lax.dot_general(a, b, NT, preferred_element_type=F32)
        s += lax.dot_general(kl[keys, :], b, NT, preferred_element_type=F32)
        s += lax.dot_general(a, ql[queries, :], NT, preferred_element_type=F32)
        return s

    def absorb(g, u, s):
        keys = pl.ds(pl.multiple_of(u * UK, UK), UK)
        m_old = m_ref[g]
        m_new = jnp.maximum(m_old, jnp.max(s, axis=0, keepdims=True))
        shrink = jnp.exp2(m_old - m_new)
        p = jnp.exp2(s - m_new)
        m_ref[g] = m_new
        l_ref[g] = l_ref[g] * shrink + jnp.sum(p, axis=0, keepdims=True)
        high = p.astype(BF16)
        low = (p - high.astype(F32)).astype(BF16)
        v = vt[:, keys]
        o = lax.dot_general(v, high, NN, preferred_element_type=F32)
        o = o[:LAB] + o[LAB:] + lax.dot_general(v[:LAB], low, NN, preferred_element_type=F32)
        acc[g] = acc[g] * shrink + o

    def exclude_self(g, u, slot):
        @pl.when((g == OWN_GROUP) & (u == 0))
        def _():
            cols = slice(OWN_COL, OWN_COL + ROWS)
            block = s_buf[slot, :ROWS, cols]
            same = lax.broadcasted_iota(jnp.int32, block.shape, 0) == lax.broadcasted_iota(jnp.int32, block.shape, 1)
            s_buf[slot, :ROWS, cols] = jnp.where(same, NEG, block)

    tiles, before, after = split_order(ORDER)
    groups, units = [t[0] for t in tiles], [t[1] for t in tiles]
    count = len(tiles)
    complete, ended = {}, []
    for step in sorted(after):
        ended += HALVES[8 * after[step]:8 * after[step] + 8]
        complete[after[step]] = [
            slot for slot, block in enumerate(BLOCKS)
            if slot != OWN and block not in ADDED and all((*block, h) in ended for h in range(2)) and all(slot not in c for c in complete.values())
        ]

    def when_step(j, parity, table, act):
        for step in range(parity, count - 2, 2):
            if table(step):
                @pl.when(j == step)
                def _(step=step):
                    act(step)

    def act_before(step):
        for item in before[step + 1]:
            event(item)

    for item in before[0]:
        event(item)
    s_buf[0] = scores(groups[0], units[0])
    exclude_self(groups[0], units[0], 0)

    def body(i, carry):
        g, u, g_next, u_next = carry
        for parity in range(2):
            j = 2 * i + parity
            when_step(j, parity, lambda step: before[step + 1], act_before)
            following = scores(g_next, u_next)
            absorb(g, u, s_buf[parity])
            s_buf[1 - parity] = following
            exclude_self(g_next, u_next, 1 - parity)
            when_step(j, parity, lambda step: step in after, lambda step: finish(after[step]))
            g, u, g_next, u_next = g_next, u_next, pick(j + 2, groups), pick(j + 2, units)
        return g, u, g_next, u_next

    lax.fori_loop(0, (count - 2) // 2, body, tuple(jnp.int32(v) for v in tiles[0] + tiles[1]))
    for item in before[count - 1]:
        event(item)
    following = scores(groups[-1], units[-1])
    absorb(groups[-2], units[-2], s_buf[0])
    s_buf[1] = following
    if count - 2 in after:
        finish(after[count - 2])
    absorb(groups[-1], units[-1], s_buf[1])
    finish(after[count - 1])

    def combined(slot, others):
        for other in others:
            home(other).wait_recv()
        top = state[slot, LAB:LAB + 1, :]
        for other in others:
            top = jnp.maximum(top, back[other, LAB:LAB + 1, :])
        weight = jnp.exp2(state[slot, LAB:LAB + 1, :] - top)
        total = state[slot, LAB + 1:LAB + 2, :] * weight
        summed = state[slot, :LAB, :] * weight
        for other in others:
            weight = jnp.exp2(back[other, LAB:LAB + 1, :] - top)
            total += back[other, LAB + 1:LAB + 2, :] * weight
            summed += back[other, :LAB, :] * weight
        return top, total, summed

    def replace(slot, values):
        state[slot, LAB:LAB + 1, :], state[slot, LAB + 1:LAB + 2, :], state[slot, :LAB, :] = values

    for block, extra in ADDED.items():
        replace(SLOT[block], combined(SLOT[block], [SLOT[b] for b in extra]))
        home(SLOT[block]).start()
    replace(OWN, combined(OWN, [SLOT[b] for b in DIRECT]))
    top, total, summed = combined(OWN, [SLOT[b] for b in ADDED])
    out[...] = 0.1 * kf[0, :ROWS, DIM:] + 0.9 * (summed / total).T

    for n in range(10):
        for link in range(4):
            plane(link, n).wait_send()
    for r in range(NR):
        for way in range(2):
            if r > 0:
                ring(way, r).wait_send()
            across(way, r).wait_send()
    for slot in range(len(BLOCKS)):
        if slot != OWN:
            home(slot).wait_send()


def body(embeddings, labels):
    vmem = pl.BlockSpec(memory_space=pltpu.VMEM)
    return pl.pallas_call(
        kernel,
        out_shape=jax.ShapeDtypeStruct((ROWS, LAB), F32),
        in_specs=[pl.BlockSpec(memory_space=pl.ANY)] * 2,
        out_specs=vmem,
        scratch_shapes=[
            pltpu.VMEM((16, ROWS, DIM), F32),
            pltpu.VMEM((NR, RING, DIM + LAB), F32),
            pltpu.VMEM((NG * GQ, DIM), BF16),
            pltpu.VMEM((NG * GQ, DIM), BF16),
            pltpu.VMEM((NU * UK, DIM), BF16),
            pltpu.VMEM((NU * UK, DIM), BF16),
            pltpu.VMEM((2 * LAB, NU * UK), BF16),
            pltpu.VMEM((2, UK, GQ), F32),
            pltpu.VMEM((NG, LAB, GQ), F32),
            pltpu.VMEM((NG, 1, GQ), F32),
            pltpu.VMEM((NG, 1, GQ), F32),
            pltpu.VMEM((16, LAB + 8, ROWS), F32),
            pltpu.VMEM((16, LAB + 8, ROWS), F32),
            pltpu.SemaphoreType.DMA((2,)),
            pltpu.SemaphoreType.DMA((4, 10)),
            pltpu.SemaphoreType.DMA((4, 10)),
            pltpu.SemaphoreType.DMA((2, NR)),
            pltpu.SemaphoreType.DMA((2, NR)),
            pltpu.SemaphoreType.DMA((2, NR)),
            pltpu.SemaphoreType.DMA((2, NR)),
            pltpu.SemaphoreType.DMA((16,)),
            pltpu.SemaphoreType.DMA((16,)),
        ],
        compiler_params=pltpu.CompilerParams(
            collective_id=0, has_side_effects=True, vmem_limit_bytes=56 * 2**20
        ),
        name="propagate",
    )(embeddings, labels)


def solution(mesh):
    placed = P(("blk", "rep"), None)
    return jax.shard_map(body, mesh=mesh, in_specs=(placed, placed), out_specs=placed, check_vma=False)
```

time: 76.8 us -> 73.2 us (0.953)
  Pallas kernels: 75.2 us -> 71.6 us
    pallas_call x1, Pallas kernels: 75.2 us -> 71.6 us  [body(): pl.pallas_call(kernel, out_shape=jax.ShapeDtypeStruct((ROWS, LAB), F32),...]
where the time goes in v2:
time: 73.2 us; the launch traced here: 73.1 us
  Pallas kernels  71.6 us (98%)
  local copies, waits for them, and re-layouts  1.47 us (2%)
    pallas_call x1, Pallas kernels, body(): pl.pallas_call(kernel, out_shape=jax.ShapeDtypeStruct((ROWS, LAB), F32),...  71.6 us
    unnamed x1, local copies, waits for them, and re-layouts  1.47 us

profile of v2, /device:TPU:1, one launch (start us, length us, event | category | flops | bytes accessed | tf_op | source)
XLA Modules:
  0.0 73.1 jit_solution(4962457862937539494)
XLA Ops:
  0.0 71.6 %propagate.1 = f32[128,128]{1,0:T(8,128)} custom-call(f32[128,768]{1,0:T(8,128)} %emb.1, f32[128,128]{1,0:T(8,128)} %lab.1), custom_call_target="tpu_custom_call" | custom-call | tf_op jit(solution)/shard_map/propagate/pallas_call | solution.py:328
  71.6 1.5 %copy.4 = f32[128,128]{1,0:T(8,128)} copy(f32[128,128]{1,0:T(8,128)} %propagate.1) | data formatting | bytes 131072

commit v3 on v2

--- a/solution.py
+++ b/solution.py
@@ -27,18 +27,19 @@
 SLOT = {block: i for i, block in enumerate(BLOCKS)}
 OWN = SLOT[(0, 0)]
 OWN_GROUP, OWN_COL = HALVES.index((0, 0, 0)) // 8, HALVES.index((0, 0, 0)) % 8 * 64
-FIRST = {(1, 1): (0, 1), (3, 3): (0, 3), (1, 3): (1, 0), (3, 1): (3, 0), (1, 2): (0, 2), (3, 2): (0, 2), (2, 1): (2, 0), (2, 3): (2, 0)}
-ADDED = {(1, 0): [(1, 1), (1, 2)], (3, 0): [(3, 3), (3, 2)], (0, 1): [(3, 1), (2, 1)], (0, 3): [(1, 3), (2, 3)]}
-DIRECT = [(2, 0), (0, 2), (2, 2)]
+FIRST = {(3, 3): (0, 3), (1, 3): (1, 0), (3, 1): (3, 0), (1, 2): (0, 2), (3, 2): (0, 2), (2, 1): (2, 0), (2, 3): (2, 0)}
+ADDED = {(1, 0): [(1, 2)], (3, 0): [(3, 3), (3, 2)], (0, 1): [(3, 1), (2, 1)], (0, 3): [(1, 3), (2, 3)]}
+DIRECT = [(2, 0), (0, 2), (2, 2), (1, 1)]
 LINKS = [("x", 1), ("x", -1), ("y", 1), ("y", -1)]
 
 ORDER = [
-    ("kc", 0), ("q", 0), ("z", 1), ("kc", 1), ("q", 1), ("qc", 0), ("t", 0, 0), ("z", 2), ("q", 2), ("kc", 2),
-    ("q", 3), ("z", 3), ("q", 4), ("qc", 1), ("kc", 3), ("t", 1, 0), ("t", 0, 1), ("z", 4), ("t", 1, 1), ("q", 5),
-    ("kc", 4), ("q", 6), ("qc", 2), ("z", 5), ("t", 2, 0), ("kc", 5), ("q", 7), ("t", 2, 1), ("t", 0, 2), ("q", 8),
-    ("z", 6), ("t", 1, 2), ("q", 9), ("kc", 6), ("qc", 3), ("t", 3, 0), ("t", 3, 1), ("z", 7), ("t", 3, 2),
-    ("kc", 7), ("t", 3, 3), ("f", 3), ("t", 1, 3), ("f", 1), ("t", 2, 2), ("t", 2, 3), ("f", 2), ("t", 0, 3),
-    ("f", 0),
+    ("kc", 0), ("qc", 4), ("q", 0), ("z", 1), ("kc", 1), ("q", 1), ("qc", 0), ("qc", 1), ("qc", 2), ("qc", 3),
+    ("t", 0, 0), ("z", 2), ("q", 2), ("kc", 2), ("q", 3), ("qc", 5), ("qc", 6), ("z", 3), ("q", 4), ("qc", 7),
+    ("kc", 3), ("t", 1, 0), ("t", 0, 1), ("z", 4), ("t", 1, 1), ("q", 5), ("kc", 4), ("q", 6), ("qc", 8), ("qc", 9),
+    ("qc", 10), ("qc", 11), ("z", 5), ("t", 2, 0), ("kc", 5), ("q", 7), ("t", 2, 1), ("t", 0, 2), ("q", 8), ("z", 6),
+    ("t", 1, 2), ("q", 9), ("kc", 6), ("qc", 12), ("qc", 13), ("qc", 14), ("qc", 15), ("t", 3, 0), ("t", 3, 1),
+    ("z", 7), ("t", 3, 2), ("kc", 7), ("t", 3, 3), ("f", 3), ("t", 2, 2), ("t", 2, 3), ("f", 2), ("t", 1, 3),
+    ("f", 1), ("t", 0, 3), ("f", 0),
 ]
 
 
@@ -151,8 +152,8 @@
         high = value.astype(BF16)
         return high, (value - high.astype(F32)).astype(BF16)
 
-    def convert_queries(g):
-        for i in range(8 * g, 8 * g + 8):
+    def convert_queries(pair):
+        for i in range(2 * pair, 2 * pair + 2):
             dx, dy, half = HALVES[i]
             rows = pl.ds(i * 64, 64)
             qh[rows, :], ql[rows, :] = halves(qf[SLOT[(dx, dy)], half * 64:half * 64 + 64])

time: 73.2 us -> 72.9 us (level)
  no operation moved by 1% of the time
where the time goes in v3:
time: 72.9 us; the launch traced here: 72.8 us
  Pallas kernels  71.3 us (98%)
  local copies, waits for them, and re-layouts  1.47 us (2%)
    pallas_call x1, Pallas kernels, body(): pl.pallas_call(kernel, out_shape=jax.ShapeDtypeStruct((ROWS, LAB), F32),...  71.3 us
    unnamed x1, local copies, waits for them, and re-layouts  1.47 us

profile of v3, /device:TPU:1, one launch (start us, length us, event | category | flops | bytes accessed | tf_op | source)
XLA Modules:
  0.0 72.8 jit_solution(10460152365504012965)
XLA Ops:
  0.0 71.3 %propagate.1 = f32[128,128]{1,0:T(8,128)} custom-call(f32[128,768]{1,0:T(8,128)} %emb.1, f32[128,128]{1,0:T(8,128)} %lab.1), custom_call_target="tpu_custom_call" | custom-call | tf_op jit(solution)/shard_map/propagate/pallas_call | solution.py:329
  71.3 1.5 %copy.4 = f32[128,128]{1,0:T(8,128)} copy(f32[128,128]{1,0:T(8,128)} %propagate.1) | data formatting | bytes 131072

commit v4 on v3

--- a/solution.py
+++ b/solution.py
@@ -36,10 +36,10 @@
     ("kc", 0), ("qc", 4), ("q", 0), ("z", 1), ("kc", 1), ("q", 1), ("qc", 0), ("qc", 1), ("qc", 2), ("qc", 3),
     ("t", 0, 0), ("z", 2), ("q", 2), ("kc", 2), ("q", 3), ("qc", 5), ("qc", 6), ("z", 3), ("q", 4), ("qc", 7),
     ("kc", 3), ("t", 1, 0), ("t", 0, 1), ("z", 4), ("t", 1, 1), ("q", 5), ("kc", 4), ("q", 6), ("qc", 8), ("qc", 9),
-    ("qc", 10), ("qc", 11), ("z", 5), ("t", 2, 0), ("kc", 5), ("q", 7), ("t", 2, 1), ("t", 0, 2), ("q", 8), ("z", 6),
-    ("t", 1, 2), ("q", 9), ("kc", 6), ("qc", 12), ("qc", 13), ("qc", 14), ("qc", 15), ("t", 3, 0), ("t", 3, 1),
-    ("z", 7), ("t", 3, 2), ("kc", 7), ("t", 3, 3), ("f", 3), ("t", 2, 2), ("t", 2, 3), ("f", 2), ("t", 1, 3),
-    ("f", 1), ("t", 0, 3), ("f", 0),
+    ("qc", 10), ("qc", 11), ("z", 5), ("t", 2, 0), ("kc", 5), ("q", 7), ("t", 2, 1), ("t", 0, 2), ("z", 6),
+    ("t", 1, 2), ("kc", 6), ("qc", 12), ("q", 8), ("qc", 13), ("qc", 14), ("q", 9), ("qc", 15), ("t", 3, 0),
+    ("t", 3, 1), ("z", 7), ("t", 3, 2), ("kc", 7), ("t", 3, 3), ("f", 3), ("t", 2, 2), ("t", 2, 3), ("f", 2),
+    ("t", 1, 3), ("f", 1), ("t", 0, 3), ("f", 0),
 ]
 
 

time: 72.9 us -> 72.9 us (level)
  no operation moved by 1% of the time
where the time goes in v4:
time: 72.9 us; the launch traced here: 72.7 us
  Pallas kernels  71.3 us (98%)
  local copies, waits for them, and re-layouts  1.47 us (2%)
    pallas_call x1, Pallas kernels, body(): pl.pallas_call(kernel, out_shape=jax.ShapeDtypeStruct((ROWS, LAB), F32),...  71.3 us
    unnamed x1, local copies, waits for them, and re-layouts  1.47 us

profile of v4, /device:TPU:1, one launch (start us, length us, event | category | flops | bytes accessed | tf_op | source)
XLA Modules:
  0.0 72.7 jit_solution(5181749803117699445)
XLA Ops:
  0.0 71.3 %propagate.1 = f32[128,128]{1,0:T(8,128)} custom-call(f32[128,768]{1,0:T(8,128)} %emb.1, f32[128,128]{1,0:T(8,128)} %lab.1), custom_call_target="tpu_custom_call" | custom-call | tf_op jit(solution)/shard_map/propagate/pallas_call | solution.py:329
  71.3 1.5 %copy.4 = f32[128,128]{1,0:T(8,128)} copy(f32[128,128]{1,0:T(8,128)} %propagate.1) | data formatting | bytes 131072
